TPU v7x, 256 devices: a whole 4x4x8 slice. The times are simulated.
256 devices in a mesh: bx: 16 (over z, y_lo), by: 4 (over x), view: 4 (over y_hi, core).
Axes of the slice: x: 4, y: 4 (y_hi: 2, y_lo: 2; y = y_hi * 2 + y_lo), z: 8, core: 2. Of those that a mesh axis runs over, the one named last changes fastest.
Arguments:
- estimate: float32 [512, 128, 128], P('bx', 'by'), may hold values from 0.5 to 2
- views_raw: float32 [4, 512, 128, 128], P('view', 'bx', 'by'), as said below
- psf_taps: float32 [4, 3, 31], P('view'), may hold values from 0.05 to 1
- offsets: int32 [4, 16, 4, 3], P('view', 'bx', 'by'), may hold values from -8 to 8
- view_weights: int32 [4, 16, 4], P(None, 'bx', 'by'), may hold values from 1 to 8
Outputs:
- estimate_next: float32 [512, 128, 128], P('bx', 'by')
Inputs may be any that keep to these rules, and one draw needn't show every extreme that they name: `views_raw`: every entry is positive.
All inputs are finite; a program needn't handle non-finite values.
Results may differ from a plain program's by a relative error of at most 0.0003.
Values sent between devices are 32-bit elements; how exact they have to be, the bound alone decides.
A program may use at most 128 MiB of HBM per device.

v0:
```python
import functools

import jax
import jax.numpy as jnp
from jax import lax
from jax.experimental import pallas as pl
from jax.experimental.pallas import tpu as pltpu
from jax.sharding import PartitionSpec as P

ITERS = 2
TAPS = 31
HALF = 15
SHIFT = 8
VIEWS = 4
CX, CY, CZ = 32, 32, 128
PX, PY = 16, 16
WIDE_X = PX + 2 * HALF
WIDE_Y = 3 * PY
N_SEMS = 128
MESH = pl.DeviceIdType.MESH


def split(value):
    high = value.astype(jnp.bfloat16)
    low = (value - high.astype(jnp.float32)).astype(jnp.bfloat16)
    return high, low


def kernel(
    sizes,
    est, view, psf_hbm, off_hbm, wts_hbm,
    out,
    raw_x, raw_y, x_wide, y_wide, value, summed, result, psf, off, wts, wide, own_aligned, aligned, own_params, params,
    taps, band_y, band_z,
    send_sem, recv_sem, local_sem,
):
    nz, nx = sizes
    bx, by, vw = lax.axis_index("bx"), lax.axis_index("by"), lax.axis_index("view")
    zc, y_lo = lax.div(bx, 2), lax.rem(bx, 2)
    y_hi, core = lax.div(vw, 2), lax.rem(vw, 2)
    y = 2 * y_hi + y_lo
    other = 1 - core
    pos = jnp.where(lax.rem(zc, 2) == 0, y, 3 - y)
    side, part = lax.div(pos, 2), lax.rem(pos, 2)
    stays = side == y_lo

    def dev(zc_, x_, y_, core_):
        return (zc_ * 2 + lax.rem(y_, 2), x_, lax.div(y_, 2) * 2 + core_)

    def chip_at(zc_, pos_):
        return jnp.where(lax.rem(zc_, 2) == 0, pos_, 3 - pos_)

    def along_x(step):
        place = lax.rem(4 * zc + pos + 4 * nz + step, 4 * nz)
        zc_, pos_ = lax.div(place, 4), lax.rem(place, 4)
        return dev(zc_, by, chip_at(zc_, pos_), core)

    def along_y(step):
        place = lax.rem(2 * by + core + 2 * nx + step, 2 * nx)
        return dev(zc, lax.div(place, 2), y, lax.rem(place, 2))

    x_left, x_right = along_x(-1), along_x(1)
    y_left, y_right = along_y(-1), along_y(1)
    first_x, last_x = (zc == 0) & (pos == 0), (zc == nz - 1) & (pos == 3)
    first_y, last_y = (by == 0) & (core == 0), (by == nx - 1) & (core == 1)

    def raw(step_x, step_y):
        return (lax.rem(bx + 2 * nz + step_x, 2 * nz), lax.rem(by + nx + step_y, nx), vw)

    far_y = dev(zc, lax.rem(by + nx + jnp.where(core == 0, -1, 1), nx), y, other)
    raw_far = raw(jnp.where(y_lo == 0, -1, 1), 0)
    barrier = pltpu.get_barrier_semaphore()
    peers = [dev(zc, by, lax.rem(y + d, 4), core) for d in (1, 2, 3)]
    peers += [dev(zc, by, lax.rem(y + d, 4), other) for d in (0, 1, 2, 3)]
    peers += [dev(lax.rem(zc + nz + d, nz), by, y, core) for d in (-1, 1)]
    peers += [far_y, raw_far, raw(0, -1), raw(0, 1)]
    for peer in peers:
        pl.semaphore_signal(barrier, inc=1, device_id=peer, device_id_type=MESH)

    used = [0]
    sent = []

    def new_sem(count=1):
        first = used[0]
        used[0] += count
        return first

    def remote(src, dst, sem, device, at=None):
        return pltpu.make_async_remote_copy(
            src_ref=src, dst_ref=dst, send_sem=send_sem.at[sem],
            recv_sem=recv_sem.at[sem if at is None else at],
            device_id=device, device_id_type=MESH)

    def go(src, dst, device):
        copy = remote(src, dst, new_sem(), device)
        copy.start()
        sent.append(copy)
        return copy

    def piece(n):
        return pl.ds(n * PX, PX)

    def spread(source_at, target, own_store):
        base = new_sem(4)
        copies = []
        for r in range(4):
            y_, core_ = chip_at(zc, 2 * y_lo + r // 2), r % 2
            me = (y_ == y) & (core_ == core)
            copy = remote(source_at(r), target(vw), base + r, dev(zc, by, y_, core_), base + vw)
            copies.append((me, copy))

        def start(chosen=range(4), last=True):
            for r in chosen:
                me, copy = copies[r]
                pl.when(jnp.logical_not(me))(copy.start)

            if last:

                @pl.when(stays)
                def _():
                    own_store()

        def wait(s):
            @pl.when(jnp.logical_not(stays & (vw == s)))
            def _():
                remote(target(s), target(s), base + s, x_left).wait_recv()

        def finish():
            for me, copy in copies:
                pl.when(jnp.logical_not(me))(copy.wait_send)

        return start, wait, finish

    local_view = pltpu.make_async_copy(
        view.at[0], wide.at[pl.ds(SHIFT, CX), pl.ds(SHIFT, CY)], local_sem.at[0])
    local_view.start()
    small = [
        pltpu.make_async_copy(src, dst, local_sem.at[2 + n])
        for n, (src, dst) in enumerate(((psf_hbm, psf), (wts_hbm, wts), (off_hbm, off)))
    ]
    for copy in small:
        copy.start()
    own_block = raw_x.at[0, pl.ds(HALF, PX)]
    local_est = pltpu.make_async_copy(
        est.at[piece(part), piece(core)], own_block, local_sem.at[1])
    pl.when(stays)(local_est.start)
    pair = jnp.where(y_lo == 0, lax.rem(y + 3, 4), lax.rem(y + 1, 4))
    pair_part = lax.rem(jnp.where(lax.rem(zc, 2) == 0, pair, 3 - pair), 2)
    est_copy = remote(
        est.at[piece(pair_part), piece(core)], own_block, new_sem(), dev(zc, by, pair, core))

    own_params[...] = jnp.zeros((8, 128), jnp.float32)
    for copy in small:
        copy.wait()
    row = psf[:, 0, :]
    own_params[0:3, 0:TAPS] = row / jnp.sum(row, axis=-1, keepdims=True)
    for v in range(VIEWS):
        own_params[4 + v : 5 + v, :] = jnp.full((1, 128), wts[0, 0, v].astype(jnp.float32))

    def store_params():
        params[vw] = own_params[...]

    params_start, params_wait, params_finish = spread(
        lambda r: own_params, lambda s: params.at[s], store_params)

    pl.semaphore_wait(barrier, len(peers))
    raw_copies, outer_copies = [], []
    low, high = pl.ds(0, SHIFT), pl.ds(CX - SHIFT, SHIFT)
    inner_rows, all_rows = pl.ds(SHIFT, CY - 2 * SHIFT), pl.ds(0, CY)
    to_low, to_high = pl.ds(0, SHIFT), pl.ds(SHIFT + CX, SHIFT)

    def send_raw(planes, rows, to_planes, to_rows, device):
        return go(view.at[0, planes, rows], wide.at[to_planes, to_rows], device)

    x_moves = ((low, to_high, raw(-1, 0)), (high, to_low, raw(1, 0)))
    for planes, to_planes, device in x_moves:
        for start in (0, CY - SHIFT):
            outer_copies.append(send_raw(
                planes, pl.ds(start, SHIFT), to_planes, pl.ds(SHIFT + start, SHIFT), device))
    for planes, to_planes, device in x_moves:
        raw_copies.append(send_raw(
            planes, inner_rows, to_planes, pl.ds(2 * SHIFT, CY - 2 * SHIFT), device))
    for rows, to_rows, device in ((low, to_high, raw(0, -1)), (high, to_low, raw(0, 1))):
        raw_copies.append(send_raw(all_rows, rows, pl.ds(SHIFT, CX), to_rows, device))
    pl.when(jnp.logical_not(stays))(est_copy.start)
    params_start()

    def send_x(field):
        return [
            go(field.at[pl.ds(HALF, HALF)], field.at[pl.ds(HALF + PX, HALF)], x_left),
            go(field.at[pl.ds(PX, HALF)], field.at[pl.ds(0, HALF)], x_right),
        ]

    def wait_x(field, copies):
        for copy in copies:
            copy.wait_recv()

        @pl.when(first_x)
        def _():
            field[0:HALF] = jnp.zeros((HALF, PY, CZ), jnp.float32)

        @pl.when(last_x)
        def _():
            field[HALF + PX : WIDE_X] = jnp.zeros((HALF, PY, CZ), jnp.float32)

    def send_y(field):
        own = field.at[:, pl.ds(PY, PY)]
        return [
            go(own, field.at[:, pl.ds(2 * PY, PY)], y_left),
            go(own, field.at[:, pl.ds(0, PY)], y_right),
        ]

    pl.when(stays)(local_est.wait)
    pl.when(jnp.logical_not(stays))(est_copy.wait)

    def send_current(iteration):
        if iteration == 0:
            return [], send_x(raw_x.at[iteration])
        raw_y[iteration, :, PY : 2 * PY, :] = raw_x[iteration, HALF : HALF + PX]
        return send_y(raw_y.at[iteration]), send_x(raw_x.at[iteration])

    current_copies = send_current(0)

    for copy in outer_copies:
        copy.wait_recv()
    for planes in (to_low, to_high):
        for rows, to_rows, device in (
            (pl.ds(SHIFT, SHIFT), to_high, raw(0, -1)),
            (pl.ds(CY, SHIFT), to_low, raw(0, 1)),
        ):
            raw_copies.append(go(wide.at[planes, rows], wide.at[planes, to_rows], device))

    for s in range(VIEWS):
        params_wait(s)

    def build(v, carry):
        for t in range(TAPS):
            taps[v, t] = jnp.broadcast_to(params[v, 0:1, t : t + 1], (8, CZ))
        r = lax.broadcasted_iota(jnp.int32, (PY, 3 * WIDE_Y), 0)
        c = lax.broadcasted_iota(jnp.int32, (PY, 3 * WIDE_Y), 1)
        group, c = lax.div(c, WIDE_Y), lax.rem(c, WIDE_Y)
        distance = c - r - 1
        outside = (first_y & (c < PY)) | (last_y & (c >= 2 * PY))
        forward = jnp.zeros((PY, 3 * WIDE_Y), jnp.float32)
        backward = forward
        for t in range(TAPS):
            tap = params[v, 1:2, t : t + 1]
            forward = jnp.where(distance == t, tap, forward)
            backward = jnp.where(distance == TAPS - 1 - t, tap, backward)
        for k, band in enumerate((forward, backward)):
            upper, lower = split(jnp.where(outside, 0.0, band))
            band_y[k, v] = jnp.where(
                group < 2, upper.astype(jnp.float32), lower.astype(jnp.float32)).astype(jnp.bfloat16)
        r = lax.broadcasted_iota(jnp.int32, (CZ, CZ), 0)
        c = lax.broadcasted_iota(jnp.int32, (CZ, CZ), 1)
        distance = r - c + HALF
        forward = jnp.zeros((CZ, CZ), jnp.float32)
        backward = forward
        for t in range(TAPS):
            tap = params[v, 2:3, t : t + 1]
            forward = jnp.where(distance == t, tap, forward)
            backward = jnp.where(distance == TAPS - 1 - t, tap, backward)
        for k, band in enumerate((forward, backward)):
            upper, lower = split(band)
            for n in range(2):
                band_z[k, v, n * CZ : (n + 1) * CZ, 0:CZ] = upper
                band_z[k, v, n * CZ : (n + 1) * CZ, CZ : 2 * CZ] = lower
        return carry

    lax.fori_loop(0, VIEWS, build, 0)

    def conv_x(field, v, k, target, row):
        def tile(j, carry):
            weights = [taps[v, TAPS - 1 - t if k else t] for t in range(TAPS)]
            sums = [None] * PX
            for a in range(WIDE_X):
                value = field[a, pl.ds(pl.multiple_of(8 * j, 8), 8), :]
                for i in range(PX):
                    if 0 <= a - i < TAPS:
                        term = weights[a - i] * value
                        sums[i] = term if sums[i] is None else sums[i] + term
            for i in range(PX):
                target[i, pl.ds(pl.multiple_of(row + 8 * j, 8), 8), :] = sums[i]
            return carry

        lax.fori_loop(0, PY // 8, tile, 0)

    def conv_y(field, v, k):
        blocks = []
        for p in range(0, PX, 2):
            both = jnp.concatenate([field[p], field[p + 1]], axis=1)
            upper, lower = split(both)
            stacked = jnp.concatenate([upper, lower, upper], axis=0)
            both = jnp.dot(band_y[k, v], stacked, preferred_element_type=jnp.float32)
            blocks += [both[:, :CZ], both[:, CZ:]]
        return jnp.concatenate(blocks, axis=0)

    def conv_z(value, v, k):
        both = jnp.concatenate(split(value), axis=1)
        both = jnp.dot(both, band_z[k, v], preferred_element_type=jnp.float32)
        return both[:, :CZ] + both[:, CZ:]

    def store_aligned():
        aligned[vw] = own_aligned[piece(part), piece(core), :]

    aligned_start, aligned_wait, aligned_finish = spread(
        lambda r: own_aligned.at[piece(r // 2), piece(r % 2)], lambda s: aligned.at[s], store_aligned)

    def align():
        local_view.wait()
        for copy in raw_copies:
            copy.wait_recv()
        ox, oy, oz = off[0, 0, 0, 0], off[0, 0, 0, 1], off[0, 0, 0, 2]
        gy = by * CY + oy + lax.broadcasted_iota(jnp.int32, (CY, CZ), 0)
        gz = oz + lax.broadcasted_iota(jnp.int32, (CY, CZ), 1)
        inside = (gy >= 0) & (gy < nx * CY) & (gz >= 0) & (gz < CZ)
        turn = lax.rem(CZ - oz, CZ)

        def planes(n, carry):
            for i in range(8):
                p = 8 * n + i
                value = wide[SHIFT + ox + p, pl.ds(SHIFT + oy, CY), :]
                value = pltpu.roll(value, turn, 1)
                gx = bx * CX + ox + p
                ok = inside & (gx >= 0) & (gx < 2 * nz * CX)
                own_aligned[p] = jnp.where(ok, value, -1.0)
            return carry

        for n in range(2):
            lax.fori_loop(2 * n, 2 * n + 2, planes, 0)
            pl.when(core == 0)(functools.partial(aligned_start, (2 * n, 2 * n + 1), n == 1))

    weights = params[0, 4:8, :]
    total = jnp.sum(weights, axis=0, keepdims=True)


    def begin_x(iteration, k, v, source):
        field = x_wide.at[iteration, k, v]
        field[HALF : HALF + PX] = source.reshape(PX, PY, CZ)
        return send_x(field)

    def begin_y(iteration, k, v, source):
        field = y_wide.at[iteration, k, v]
        field[:, PY : 2 * PY, :] = source.reshape(PX, PY, CZ)
        return send_y(field)

    def end_x(iteration, k, v, copies):
        field = x_wide.at[iteration, k, v]
        wait_x(field, copies)
        conv_x(field, v, k, value.at[v], 0)
        return value[v].reshape(PX * PY, CZ)

    def end_y(iteration, k, v, copies):
        for copy in copies:
            copy.wait_recv()
        return conv_y(y_wide.at[iteration, k, v], v, k)

    for iteration in range(ITERS):
        if iteration == 0:
            x_first, x_first_back = (True,) * VIEWS, (True, True, False, False)
            order, order_back = (0, 2, 1, 3), (2, 0, 3, 1)
            align()
        else:
            x_first, x_first_back = (True, True, False, False), (False, False, True, True)
            order, order_back = (2, 0, 1, 3), (0, 2, 1, 3)
        copies = {}
        for copy in current_copies[0]:
            copy.wait_recv()
        for v in range(VIEWS):
            if not x_first[v]:
                copies[v] = begin_x(iteration, 0, v, conv_y(raw_y.at[iteration], v, 0))
        wait_x(raw_x.at[iteration], current_copies[1])
        for v in range(VIEWS):
            if x_first[v]:
                field = y_wide.at[iteration, 0, v]
                conv_x(raw_x.at[iteration], v, 0, field, PY)
                copies[v] = send_y(field)
        if iteration == 0:
            pl.when(core == 1)(aligned_start)
        for v in order:
            blurred = (end_y if x_first[v] else end_x)(iteration, 0, v, copies[v])
            blurred = conv_z(blurred, v, 0)
            if iteration == 0:
                aligned_wait(v)
            recorded = aligned[v].reshape(PX * PY, CZ)
            ratio = jnp.where(recorded >= 0.0, recorded / blurred, 1.0)
            back = conv_z(ratio, v, 1)
            copies[v] = (begin_x if x_first_back[v] else begin_y)(iteration, 1, v, back)
        for v in order_back:
            if x_first_back[v]:
                wait_x(x_wide.at[iteration, 1, v], copies[v])
                field = y_wide.at[iteration, 1, v]
                conv_x(x_wide.at[iteration, 1, v], v, 1, field, PY)
                copies[v] = send_y(field)
            else:
                copies[v] = begin_x(iteration, 1, v, end_y(iteration, 1, v, copies[v]))
        for n, v in enumerate(order_back):
            back = (end_y if x_first_back[v] else end_x)(iteration, 1, v, copies[v])
            term = params[0, 4 + v : 5 + v, :] * jnp.log(back)
            summed[...] = term if n == 0 else summed[...] + term
        update = jnp.exp(summed[...] / total).reshape(PX, PY, CZ)
        updated = raw_x[iteration, HALF : HALF + PX] * update
        if iteration + 1 < ITERS:
            raw_x[iteration + 1, HALF : HALF + PX] = updated
            current_copies = send_current(iteration + 1)
        else:
            result[...] = updated

    shared = PX // 2
    own_target = out.at[piece(part), piece(core)]
    chip_mate = dev(zc, by, y, other)
    base = new_sem(4)
    mate_copy = remote(result, own_target, new_sem(), chip_mate)
    results = []
    for n in range(2):
        y_ = side + 2 * n
        for c in range(2):
            copy = remote(
                result.at[pl.ds(c * shared, shared)],
                out.at[pl.ds(part * PX + c * shared, shared), piece(core)],
                base + 2 * n + c, dev(zc, by, y_, c), base + 2 * part + core)
            results.append((y_ != y, copy))
    for away, copy in results:
        pl.when(away)(copy.start)

    @pl.when(stays)
    def _():
        mate_copy.start()
        own_target[...] = result[...]

    params_finish()
    aligned_finish()
    for copy in sent:
        copy.wait_send()

    base_mate = new_sem(4)
    forwards = []
    for s in (2, 3, 0, 1):
        away = chip_at(zc, 2 * y_lo + s // 2) != y
        got, missing = [
            out.at[pl.ds(s // 2 * PX + c * shared, shared), piece(s % 2)] for c in (core, other)
        ]
        arrival = remote(got, got, base + s, x_left)
        forward = remote(got, got, base_mate + s, chip_mate)
        missed = remote(missing, missing, base_mate + s, chip_mate)

        @pl.when(away)
        def _(arrival=arrival, forward=forward):
            arrival.wait_recv()
            forward.start()

        forwards.append((away, forward, missed))

    @pl.when(stays)
    def _():
        mate_copy.wait()

    for away, forward, missed in forwards:

        @pl.when(away)
        def _(forward=forward, missed=missed):
            missed.wait_recv()
            forward.wait_send()

    for away, copy in results:
        pl.when(away)(copy.wait_send)


def solution(mesh):
    nz, nx = mesh.shape["bx"] // 2, mesh.shape["by"]
    f32, bf16 = jnp.float32, jnp.bfloat16

    def shards(estimate, views_raw, psf_taps, offsets, view_weights):
        vmem = pl.BlockSpec(memory_space=pltpu.VMEM)
        hbm = pl.BlockSpec(memory_space=pltpu.HBM)
        return pl.pallas_call(
            functools.partial(kernel, (nz, nx)),
            out_shape=jax.ShapeDtypeStruct((CX, CY, CZ), f32),
            in_specs=[hbm] * 5,
            out_specs=vmem,
            scratch_shapes=[
                pltpu.VMEM((ITERS, WIDE_X, PY, CZ), f32),
                pltpu.VMEM((ITERS, PX, WIDE_Y, CZ), f32),
                pltpu.VMEM((ITERS, 2, VIEWS, WIDE_X, PY, CZ), f32),
                pltpu.VMEM((ITERS, 2, VIEWS, PX, WIDE_Y, CZ), f32),
                pltpu.VMEM((VIEWS, PX, PY, CZ), f32),
                pltpu.VMEM((PX * PY, CZ), f32),
                pltpu.VMEM((PX, PY, CZ), f32),
                pltpu.VMEM((3, 1, TAPS), f32),
                pltpu.SMEM((1, 1, 1, 3), jnp.int32),
                pltpu.SMEM((1, 1, VIEWS), jnp.int32),
                pltpu.VMEM((CX + 2 * SHIFT, CY + 2 * SHIFT, CZ), f32),
                pltpu.VMEM((CX, CY, CZ), f32),
                pltpu.VMEM((VIEWS, PX, PY, CZ), f32),
                pltpu.VMEM((8, 128), f32),
                pltpu.VMEM((VIEWS, 8, 128), f32),
                pltpu.VMEM((VIEWS, TAPS, 8, CZ), f32),
                pltpu.VMEM((2, VIEWS, PY, 3 * WIDE_Y), bf16),
                pltpu.VMEM((2, VIEWS, 2 * CZ, 2 * CZ), bf16),
                pltpu.SemaphoreType.DMA((N_SEMS,)),
                pltpu.SemaphoreType.DMA((N_SEMS,)),
                pltpu.SemaphoreType.DMA((5,)),
            ],
            compiler_params=pltpu.CompilerParams(
                collective_id=0, has_side_effects=True, vmem_limit_bytes=53 * 1024 * 1024
            ),
            cost_estimate=pl.CostEstimate(flops=10**9, bytes_accessed=2 * 10**6, transcendentals=10**6),
        )(
            estimate,
            views_raw,
            jnp.transpose(psf_taps, (1, 0, 2)),
            offsets,
            jnp.transpose(view_weights, (1, 2, 0)),
        )

    return jax.shard_map(
        shards,
        mesh=mesh,
        in_specs=(
            P("bx", "by", None),
            P("view", "bx", "by", None),
            P("view", None, None),
            P("view", "bx", "by", None),
            P(None, "bx", "by"),
        ),
        out_specs=P("bx", "by", None),
        check_vma=False,
    )
```

profile of v0, /device:TPU:17, one launch (start us, length us, event | category | flops | bytes accessed | tf_op | source)
XLA Modules:
  0.0 72.4 jit_solution(12771841406663670918)
XLA Ops:
  0.0 0.0 copy-start
  0.0 0.0 copy-start.1
  0.0 0.0 copy-start.2
  0.0 0.7 copy-done
  0.7 0.0 copy-done.1
  0.7 0.0 copy-done.2
  0.7 70.9 %shard_map.55 = f32[32,32,128]{2,1,0:T(8,128)S(1)} custom-call(f32[32,32,128]{2,1,0:T(8,128)} %est.1, f32[1,32,32,128]{3,2,1,0:T(8,128)} %view.1, f32[3,1,31]{2,1,0:T(1,128)S(1)} %bitcast.2, s32[1,1,1,3]{3,2,1,0:T(1,128)S(1)} %copy-done.1, s32[1,1,4]{2,1,0:T(1,128)S(1)} %bitcast.3), custom_call_target="tpu_custom_call" | custom-call | flops 1000000000 | bytes 2000000 | tf_op jit(solution)/shard_map/pallas_call | solution.py:476
  71.6 0.8 %copy.7 = f32[32,32,128]{2,1,0:T(8,128)} copy(f32[32,32,128]{2,1,0:T(8,128)S(1)} %shard_map.55) | data formatting | bytes 1048576
Async XLA Ops:
  0.0 0.7 copy-start
  0.0 0.7 copy-start.1
  0.0 0.7 copy-start.2
where the time goes:
time: 72.8 us; the launch traced here: 72.4 us
  Pallas kernels  70.9 us (97%)
  local copies, waits for them, and re-layouts  1.48 us (2%)
    pallas_call x1, Pallas kernels, shards(): pl.pallas_call(functools.partial(kernel, (nz, nx)), out_shape=jax.ShapeDt...  70.9 us
    unnamed x7, local copies, waits for them, and re-layouts  1.48 us

commit v1 on v0

--- a/solution.py
+++ b/solution.py
@@ -164,6 +164,8 @@
         lambda r: own_params, lambda s: params.at[s], store_params)
 
     pl.semaphore_wait(barrier, len(peers))
+    pl.when(jnp.logical_not(stays))(est_copy.start)
+    params_start()
     raw_copies, outer_copies = [], []
     low, high = pl.ds(0, SHIFT), pl.ds(CX - SHIFT, SHIFT)
     inner_rows, all_rows = pl.ds(SHIFT, CY - 2 * SHIFT), pl.ds(0, CY)
@@ -182,8 +184,6 @@
             planes, inner_rows, to_planes, pl.ds(2 * SHIFT, CY - 2 * SHIFT), device))
     for rows, to_rows, device in ((low, to_high, raw(0, -1)), (high, to_low, raw(0, 1))):
         raw_copies.append(send_raw(all_rows, rows, pl.ds(SHIFT, CX), to_rows, device))
-    pl.when(jnp.logical_not(stays))(est_copy.start)
-    params_start()
 
     def send_x(field):
         return [
@@ -285,9 +285,9 @@
 
         lax.fori_loop(0, PY // 8, tile, 0)
 
-    def conv_y(field, v, k):
+    def conv_y(field, v, k, planes=(0, PX)):
         blocks = []
-        for p in range(0, PX, 2):
+        for p in range(*planes, 2):
             both = jnp.concatenate([field[p], field[p + 1]], axis=1)
             upper, lower = split(both)
             stacked = jnp.concatenate([upper, lower, upper], axis=0)
@@ -327,11 +327,27 @@
             return carry
 
         for n in range(2):
-            lax.fori_loop(2 * n, 2 * n + 2, planes, 0)
+            planes(2 * n, 0)
+            planes(2 * n + 1, 0)
             pl.when(core == 0)(functools.partial(aligned_start, (2 * n, 2 * n + 1), n == 1))
 
     weights = params[0, 4:8, :]
     total = jnp.sum(weights, axis=0, keepdims=True)
+
+    shared = PX // 2
+    own_target = out.at[piece(part), piece(core)]
+    chip_mate = dev(zc, by, y, other)
+    base = new_sem(4)
+    mate_copy = remote(result, own_target, new_sem(), chip_mate)
+    results = []
+    for n in range(2):
+        y_ = side + 2 * n
+        for c in range(2):
+            copy = remote(
+                result.at[pl.ds(c * shared, shared)],
+                out.at[pl.ds(part * PX + c * shared, shared), piece(core)],
+                base + 2 * n + c, dev(zc, by, y_, c), base + 2 * part + core)
+            results.append((y_ != y, copy))
 
 
     def begin_x(iteration, k, v, source):
@@ -394,34 +410,30 @@
                 copies[v] = send_y(field)
             else:
                 copies[v] = begin_x(iteration, 1, v, end_y(iteration, 1, v, copies[v]))
+        last = order_back[-1] if iteration + 1 == ITERS else None
         for n, v in enumerate(order_back):
+            if v == last:
+                break
             back = (end_y if x_first_back[v] else end_x)(iteration, 1, v, copies[v])
             term = params[0, 4 + v : 5 + v, :] * jnp.log(back)
             summed[...] = term if n == 0 else summed[...] + term
-        update = jnp.exp(summed[...] / total).reshape(PX, PY, CZ)
-        updated = raw_x[iteration, HALF : HALF + PX] * update
-        if iteration + 1 < ITERS:
-            raw_x[iteration + 1, HALF : HALF + PX] = updated
+        if last is None:
+            update = jnp.exp(summed[...] / total).reshape(PX, PY, CZ)
+            raw_x[iteration + 1, HALF : HALF + PX] = raw_x[iteration, HALF : HALF + PX] * update
             current_copies = send_current(iteration + 1)
-        else:
-            result[...] = updated
-
-    shared = PX // 2
-    own_target = out.at[piece(part), piece(core)]
-    chip_mate = dev(zc, by, y, other)
-    base = new_sem(4)
-    mate_copy = remote(result, own_target, new_sem(), chip_mate)
-    results = []
-    for n in range(2):
-        y_ = side + 2 * n
+            continue
+        for copy in copies[last]:
+            copy.wait_recv()
         for c in range(2):
-            copy = remote(
-                result.at[pl.ds(c * shared, shared)],
-                out.at[pl.ds(part * PX + c * shared, shared), piece(core)],
-                base + 2 * n + c, dev(zc, by, y_, c), base + 2 * part + core)
-            results.append((y_ != y, copy))
-    for away, copy in results:
-        pl.when(away)(copy.start)
+            planes = (c * shared, (c + 1) * shared)
+            back = conv_y(y_wide.at[iteration, 1, last], last, 1, planes)
+            term = params[0, 4 + last : 5 + last, :] * jnp.log(back)
+            log_sum = summed[planes[0] * PY : planes[1] * PY, :] + term
+            update = jnp.exp(log_sum / total).reshape(shared, PY, CZ)
+            result[planes[0] : planes[1]] = (
+                raw_x[iteration, HALF + planes[0] : HALF + planes[1]] * update)
+            for away, copy in results[c::2]:
+                pl.when(away)(copy.start)
 
     @pl.when(stays)
     def _():

time: 72.8 us -> 72.5 us (level)
  no operation moved by 1% of the time
where the time goes in v1:
time: 72.5 us; the launch traced here: 72.4 us
  Pallas kernels  70.9 us (98%)
  local copies, waits for them, and re-layouts  1.48 us (2%)
    pallas_call x1, Pallas kernels, shards(): pl.pallas_call(functools.partial(kernel, (nz, nx)), out_shape=jax.ShapeDt...  70.9 us
    unnamed x7, local copies, waits for them, and re-layouts  1.48 us

profile of v1, /device:TPU:17, one launch (start us, length us, event | category | flops | bytes accessed | tf_op | source)
XLA Modules:
  0.0 72.4 jit_solution(17854312386679260479)
XLA Ops:
  0.0 0.0 copy-start
  0.0 0.0 copy-start.1
  0.0 0.0 copy-start.2
  0.0 0.7 copy-done
  0.7 0.0 copy-done.1
  0.7 0.0 copy-done.2
  0.7 70.9 %shard_map.55 = f32[32,32,128]{2,1,0:T(8,128)S(1)} custom-call(f32[32,32,128]{2,1,0:T(8,128)} %est.1, f32[1,32,32,128]{3,2,1,0:T(8,128)} %view.1, f32[3,1,31]{2,1,0:T(1,128)S(1)} %bitcast.2, s32[1,1,1,3]{3,2,1,0:T(1,128)S(1)} %copy-done.1, s32[1,1,4]{2,1,0:T(1,128)S(1)} %bitcast.3), custom_call_target="tpu_custom_call" | custom-call | flops 1000000000 | bytes 2000000 | tf_op jit(solution)/shard_map/pallas_call | solution.py:488
  71.6 0.8 %copy.7 = f32[32,32,128]{2,1,0:T(8,128)} copy(f32[32,32,128]{2,1,0:T(8,128)S(1)} %shard_map.55) | data formatting | bytes 1048576
Async XLA Ops:
  0.0 0.7 copy-start
  0.0 0.7 copy-start.1
  0.0 0.7 copy-start.2

commit v2 on v1

--- a/solution.py
+++ b/solution.py
@@ -203,23 +203,18 @@
         def _():
             field[HALF + PX : WIDE_X] = jnp.zeros((HALF, PY, CZ), jnp.float32)
 
-    def send_y(field):
-        own = field.at[:, pl.ds(PY, PY)]
+    def send_y(field, start=0, count=PX):
+        planes = pl.ds(start, count)
+        own = field.at[planes, pl.ds(PY, PY)]
         return [
-            go(own, field.at[:, pl.ds(2 * PY, PY)], y_left),
-            go(own, field.at[:, pl.ds(0, PY)], y_right),
+            go(own, field.at[planes, pl.ds(2 * PY, PY)], y_left),
+            go(own, field.at[planes, pl.ds(0, PY)], y_right),
         ]
 
     pl.when(stays)(local_est.wait)
     pl.when(jnp.logical_not(stays))(est_copy.wait)
 
-    def send_current(iteration):
-        if iteration == 0:
-            return [], send_x(raw_x.at[iteration])
-        raw_y[iteration, :, PY : 2 * PY, :] = raw_x[iteration, HALF : HALF + PX]
-        return send_y(raw_y.at[iteration]), send_x(raw_x.at[iteration])
-
-    current_copies = send_current(0)
+    current_copies = [], send_x(raw_x.at[0])
 
     for copy in outer_copies:
         copy.wait_recv()
@@ -410,30 +405,33 @@
                 copies[v] = send_y(field)
             else:
                 copies[v] = begin_x(iteration, 1, v, end_y(iteration, 1, v, copies[v]))
-        last = order_back[-1] if iteration + 1 == ITERS else None
+        last = order_back[-1]
         for n, v in enumerate(order_back):
             if v == last:
                 break
             back = (end_y if x_first_back[v] else end_x)(iteration, 1, v, copies[v])
             term = params[0, 4 + v : 5 + v, :] * jnp.log(back)
             summed[...] = term if n == 0 else summed[...] + term
-        if last is None:
-            update = jnp.exp(summed[...] / total).reshape(PX, PY, CZ)
-            raw_x[iteration + 1, HALF : HALF + PX] = raw_x[iteration, HALF : HALF + PX] * update
-            current_copies = send_current(iteration + 1)
-            continue
         for copy in copies[last]:
             copy.wait_recv()
+        raw_y_sent = []
         for c in range(2):
             planes = (c * shared, (c + 1) * shared)
             back = conv_y(y_wide.at[iteration, 1, last], last, 1, planes)
             term = params[0, 4 + last : 5 + last, :] * jnp.log(back)
             log_sum = summed[planes[0] * PY : planes[1] * PY, :] + term
             update = jnp.exp(log_sum / total).reshape(shared, PY, CZ)
-            result[planes[0] : planes[1]] = (
-                raw_x[iteration, HALF + planes[0] : HALF + planes[1]] * update)
-            for away, copy in results[c::2]:
-                pl.when(away)(copy.start)
+            updated = raw_x[iteration, HALF + planes[0] : HALF + planes[1]] * update
+            if iteration + 1 < ITERS:
+                raw_y[iteration + 1, planes[0] : planes[1], PY : 2 * PY] = updated
+                raw_y_sent += send_y(raw_y.at[iteration + 1], planes[0], shared)
+                raw_x[iteration + 1, HALF + planes[0] : HALF + planes[1]] = updated
+            else:
+                result[planes[0] : planes[1]] = updated
+                for away, copy in results[c::2]:
+                    pl.when(away)(copy.start)
+        if iteration + 1 < ITERS:
+            current_copies = raw_y_sent, send_x(raw_x.at[iteration + 1])
 
     @pl.when(stays)
     def _():

time: 72.5 us -> 72.6 us (level)
  no operation moved by 1% of the time
where the time goes in v2:
time: 72.6 us; the launch traced here: 72.5 us
  Pallas kernels  71 us (98%)
  local copies, waits for them, and re-layouts  1.48 us (2%)
    pallas_call x1, Pallas kernels, shards(): pl.pallas_call(functools.partial(kernel, (nz, nx)), out_shape=jax.ShapeDt...  71 us
    unnamed x7, local copies, waits for them, and re-layouts  1.48 us

profile of v2, /device:TPU:17, one launch (start us, length us, event | category | flops | bytes accessed | tf_op | source)
XLA Modules:
  0.0 72.5 jit_solution(12049339555181995655)
XLA Ops:
  0.0 0.0 copy-start
  0.0 0.0 copy-start.1
  0.0 0.0 copy-start.2
  0.0 0.7 copy-done
  0.7 0.0 copy-done.1
  0.7 0.0 copy-done.2
  0.7 71.0 %shard_map.55 = f32[32,32,128]{2,1,0:T(8,128)S(1)} custom-call(f32[32,32,128]{2,1,0:T(8,128)} %est.1, f32[1,32,32,128]{3,2,1,0:T(8,128)} %view.1, f32[3,1,31]{2,1,0:T(1,128)S(1)} %bitcast.2, s32[1,1,1,3]{3,2,1,0:T(1,128)S(1)} %copy-done.1, s32[1,1,4]{2,1,0:T(1,128)S(1)} %bitcast.3), custom_call_target="tpu_custom_call" | custom-call | flops 1000000000 | bytes 2000000 | tf_op jit(solution)/shard_map/pallas_call | solution.py:486
  71.7 0.8 %copy.7 = f32[32,32,128]{2,1,0:T(8,128)} copy(f32[32,32,128]{2,1,0:T(8,128)S(1)} %shard_map.55) | data formatting | bytes 1048576
Async XLA Ops:
  0.0 0.7 copy-start
  0.0 0.7 copy-start.1
  0.0 0.7 copy-start.2

commit v3 on v1

--- a/solution.py
+++ b/solution.py
@@ -185,15 +185,21 @@
     for rows, to_rows, device in ((low, to_high, raw(0, -1)), (high, to_low, raw(0, 1))):
         raw_copies.append(send_raw(all_rows, rows, pl.ds(SHIFT, CX), to_rows, device))
 
+    not_first, not_last = jnp.logical_not(first_x), jnp.logical_not(last_x)
+    x_sent = []
+
     def send_x(field):
-        return [
-            go(field.at[pl.ds(HALF, HALF)], field.at[pl.ds(HALF + PX, HALF)], x_left),
-            go(field.at[pl.ds(PX, HALF)], field.at[pl.ds(0, HALF)], x_right),
-        ]
+        left = remote(
+            field.at[pl.ds(HALF, HALF)], field.at[pl.ds(HALF + PX, HALF)], new_sem(), x_left)
+        right = remote(field.at[pl.ds(PX, HALF)], field.at[pl.ds(0, HALF)], new_sem(), x_right)
+        pl.when(not_first)(left.start)
+        pl.when(not_last)(right.start)
+        x_sent.append((left, right))
+        return left, right
 
     def wait_x(field, copies):
-        for copy in copies:
-            copy.wait_recv()
+        pl.when(not_last)(copies[0].wait_recv)
+        pl.when(not_first)(copies[1].wait_recv)
 
         @pl.when(first_x)
         def _():
@@ -444,6 +450,9 @@
     aligned_finish()
     for copy in sent:
         copy.wait_send()
+    for left, right in x_sent:
+        pl.when(not_first)(left.wait_send)
+        pl.when(not_last)(right.wait_send)
 
     base_mate = new_sem(4)
     forwards = []

time: 72.5 us -> 71.2 us (0.982); the launches traced: 72.4 us -> 70.3 us
  Pallas kernels: 70.9 us -> 68.8 us
    pallas_call x1, Pallas kernels: 70.9 us -> 68.8 us  [shards(): pl.pallas_call(functools.partial(kernel, (nz, nx)), out_shape=jax.ShapeDt...]
where the time goes in v3:
time: 71.2 us; the launch traced here: 70.3 us
  Pallas kernels  68.8 us (97%)
  local copies, waits for them, and re-layouts  1.48 us (2%)
    pallas_call x1, Pallas kernels, shards(): pl.pallas_call(functools.partial(kernel, (nz, nx)), out_shape=jax.ShapeDt...  68.8 us
    unnamed x7, local copies, waits for them, and re-layouts  1.48 us

profile of v3, /device:TPU:17, one launch (start us, length us, event | category | flops | bytes accessed | tf_op | source)
XLA Modules:
  0.0 70.3 jit_solution(3757866945181314997)
XLA Ops:
  0.0 0.0 copy-start
  0.0 0.0 copy-start.1
  0.0 0.0 copy-start.2
  0.0 0.7 copy-done
  0.7 0.0 copy-done.1
  0.7 0.0 copy-done.2
  0.7 68.8 %shard_map.55 = f32[32,32,128]{2,1,0:T(8,128)S(1)} custom-call(f32[32,32,128]{2,1,0:T(8,128)} %est.1, f32[1,32,32,128]{3,2,1,0:T(8,128)} %view.1, f32[3,1,31]{2,1,0:T(1,128)S(1)} %bitcast.2, s32[1,1,1,3]{3,2,1,0:T(1,128)S(1)} %copy-done.1, s32[1,1,4]{2,1,0:T(1,128)S(1)} %bitcast.3), custom_call_target="tpu_custom_call" | custom-call | flops 1000000000 | bytes 2000000 | tf_op jit(solution)/shard_map/pallas_call | solution.py:497
  69.5 0.8 %copy.7 = f32[32,32,128]{2,1,0:T(8,128)} copy(f32[32,32,128]{2,1,0:T(8,128)S(1)} %shard_map.55) | data formatting | bytes 1048576
Async XLA Ops:
  0.0 0.7 copy-start
  0.0 0.7 copy-start.1
  0.0 0.7 copy-start.2
